TPU v7x, 32 devices: a whole 2x2x4 slice. The times are simulated.
32 devices in a mesh: clip: 2 (over x), tile: 16 (over z, y, core).
Axes of the slice: x: 2, y: 2, z: 4, core: 2. Of those that a mesh axis runs over, the one named last changes fastest.
Arguments:
- queries: bfloat16 [128, 256, 256], P(('clip', 'tile')), parts along dimension 0, may hold values from -150 to 150
- keys: bfloat16 [128, 256, 256], P(('clip', 'tile')), parts along dimension 0, may hold values from -7 to 7
- values: bfloat16 [128, 256, 256], P(('clip', 'tile')), parts along dimension 0, may hold values from -6 to 6
- counts: int32 [32], P('clip'), parts along dimension 0, may hold values from 3 to 4, as said below
- neighbors: int32 [112, 45], P('clip'), parts along dimension 0, may hold values from -1 to 55, as said below
Outputs:
- attended: bfloat16 [128, 256, 256], P(('clip', 'tile')), parts along dimension 0
There are 2 independent parts, one for each index of `clip`. A program takes and returns all parts, laid end to end along the dimension named above; each array names one. Nothing has to cross between parts.
Inputs may be any that keep to these rules, and one draw needn't show every extreme that they name: `counts`: entries sum to 56; some device owns exactly 4 tiles and some exactly 3. `neighbors`: row t lists 3 x 3 x 5 tiles: the slabs from t's slab - 1 to + 1 and the rows from t's row - 1 to + 1 (-1 where these lie outside the grid), and 5 consecutive columns inside the grid that contain t's column. So every listed id lies within 39 of t, and t lists itself.
All inputs are finite; a program needn't handle non-finite values.
Results may differ from a plain program's by a relative error of at most 0.0033.
Values may be sent and summed in bfloat16 or wider, within the bound.
A program may use at most 128 MiB of HBM per device.

v0:
```python
import jax
import jax.numpy as jnp
from jax import lax
from jax.sharding import PartitionSpec as P

HEADS = 2
NBR = 45
REACH = 13


masked_score = -1e30


def passed_along(value, axis, steps):
    count = lax.axis_size(axis)
    initial, last = (max(0, -steps), min(count, count - steps))
    return lax.ppermute(value, axis, [(source, source + steps) for source in range(initial, last)])


def per_device(queries, keys, values, counts, neighbors):
    capacity = queries.shape[0]
    tokens = queries.shape[1]
    channels = queries.shape[2]
    head_dim = channels // HEADS
    device_count = counts.shape[0]
    position = lax.axis_index("tile")
    ends = jnp.cumsum(counts)
    starts = ends - counts
    owned = counts[position]
    first_id = starts[position]
    paired = jnp.concatenate([keys, values], axis=2)
    earlier = []
    later = []
    carried_before = paired
    carried_after = paired
    for step in range(REACH):
        carried_before = passed_along(carried_before, "tile", 1)
        carried_after = passed_along(carried_after, "tile", -1)
        earlier.append(carried_before)
        later.append(carried_after)
    window = jnp.concatenate(earlier[::-1] + [paired] + later, axis=0)
    window_size = window.shape[0]
    factor = head_dim ** (-0.5)

    def attend(offset, output):
        tile_id = first_id + offset
        listed = lax.dynamic_index_in_dim(neighbors, tile_id, 0, keepdims=False)
        usable = listed >= 0
        owner_of = jnp.sum((starts[None, :] <= listed[:, None]).astype(jnp.int32), axis=1) - 1
        owner_of = jnp.clip(owner_of, 0, device_count - 1)
        places = (owner_of - position + REACH) * capacity + listed - starts[owner_of]
        places = jnp.clip(places, 0, window_size - 1)
        picked = jnp.take(window, places, axis=0)
        query_tile = lax.dynamic_index_in_dim(queries, offset, 0, keepdims=False)
        keep_keys = jnp.repeat(usable, tokens, total_repeat_length=NBR * tokens)
        results = []
        for head in range(HEADS):
            low = head * head_dim
            key_block = picked[:, :, low : low + head_dim].reshape(NBR * tokens, head_dim)
            value_block = picked[:, :, channels + low : channels + low + head_dim].reshape(
                NBR * tokens, head_dim
            )
            query_head = query_tile[:, low : low + head_dim]
            scores = (
                lax.dot_general(
                    query_head,
                    key_block,
                    (((1,), (1,)), ((), ())),
                    preferred_element_type=jnp.float32,
                )
                * factor
            )
            scores = jnp.where(keep_keys[None, :], scores, masked_score)
            highest = jnp.max(scores, axis=-1, keepdims=True)
            weights = jnp.exp(scores - highest)
            totals = jnp.sum(weights, axis=-1)
            probs = weights.astype(jnp.bfloat16)
            mixed = jnp.dot(probs, value_block, preferred_element_type=jnp.float32)
            mixed = mixed / totals[:, None]
            results.append(mixed.astype(jnp.bfloat16))
        result = jnp.concatenate(results, axis=1)
        return lax.dynamic_update_index_in_dim(output, result, offset, 0)

    blank = jnp.zeros_like(queries)
    return lax.fori_loop(0, owned, attend, blank)


def solution(mesh):
    in_specs = (
        P(("clip", "tile"), None, None),
        P(("clip", "tile"), None, None),
        P(("clip", "tile"), None, None),
        P("clip"),
        P("clip", None),
    )
    out_specs = P(("clip", "tile"), None, None)
    return jax.shard_map(
        per_device, mesh=mesh, in_specs=in_specs, out_specs=out_specs, check_vma=False
    )
```

profile of v0, /device:TPU:12, one launch (start us, length us, event | category | flops | bytes accessed | tf_op | source)
XLA Modules:
  0.0 698.8 jit_solution(3498666037455736010)
XLA Ops:
  7.8 21.8 %collective-permute-done = bf16[4,256,512]{2,1,0:T(8,128)(2,1)S(1)} collective-permute-done((bf16[4,256,512]{2,1,0:T(8,128)(2,1)S(1)}, bf16[4,256,512]{2,1,0:T(8,128)(2,1)S(1)}, u32[]{:S(2)}, u32[]{:S(2)}) %collective-permute-start) | collective-permute-done | bytes 1048608 | tf_op jit(solution)/shard_map/ppermute | solution.py:17
  31.5 8.2 %collective-permute-done.13 = bf16[4,256,512]{2,1,0:T(8,128)(2,1)S(1)} collective-permute-done((bf16[4,256,512]{2,1,0:T(8,128)(2,1)S(1)}, bf16[4,256,512]{2,1,0:T(8,128)(2,1)S(1)}, u32[]{:S(2)}, u32[]{:S(2)}) %collective-permute-start.13) | collective-permute-done | bytes 1048608 | tf_op jit(solution)/shard_map/ppermute | solution.py:17
  47.6 15.1 %collective-permute-done.14 = bf16[4,256,512]{2,1,0:T(8,128)(2,1)S(1)} collective-permute-done((bf16[4,256,512]{2,1,0:T(8,128)(2,1)S(1)}, bf16[4,256,512]{2,1,0:T(8,128)(2,1)S(1)}, u32[]{:S(2)}, u32[]{:S(2)}) %collective-permute-start.14) | collective-permute-done | bytes 1048608 | tf_op jit(solution)/shard_map/ppermute | solution.py:17
  71.3 19.8 %collective-permute-done.15 = bf16[4,256,512]{2,1,0:T(8,128)(2,1)S(1)} collective-permute-done((bf16[4,256,512]{2,1,0:T(8,128)(2,1)S(1)}, bf16[4,256,512]{2,1,0:T(8,128)(2,1)S(1)}, u32[]{:S(2)}, u32[]{:S(2)}) %collective-permute-start.15) | collective-permute-done | bytes 1048608 | tf_op jit(solution)/shard_map/ppermute | solution.py:17
  98.6 19.8 %collective-permute-done.16 = bf16[4,256,512]{2,1,0:T(8,128)(2,1)S(1)} collective-permute-done((bf16[4,256,512]{2,1,0:T(8,128)(2,1)S(1)}, bf16[4,256,512]{2,1,0:T(8,128)(2,1)S(1)}, u32[]{:S(2)}, u32[]{:S(2)}) %collective-permute-start.16) | collective-permute-done | bytes 1048608 | tf_op jit(solution)/shard_map/ppermute | solution.py:17
  126.0 20.8 %collective-permute-done.17 = bf16[4,256,512]{2,1,0:T(8,128)(2,1)S(1)} collective-permute-done((bf16[4,256,512]{2,1,0:T(8,128)(2,1)S(1)}, bf16[4,256,512]{2,1,0:T(8,128)(2,1)S(1)}, u32[]{:S(2)}, u32[]{:S(2)}) %collective-permute-start.17) | collective-permute-done | bytes 1048608 | tf_op jit(solution)/shard_map/ppermute | solution.py:17
  153.3 20.8 %collective-permute-done.18 = bf16[4,256,512]{2,1,0:T(8,128)(2,1)S(1)} collective-permute-done((bf16[4,256,512]{2,1,0:T(8,128)(2,1)S(1)}, bf16[4,256,512]{2,1,0:T(8,128)(2,1)S(1)}, u32[]{:S(2)}, u32[]{:S(2)}) %collective-permute-start.18) | collective-permute-done | bytes 1048608 | tf_op jit(solution)/shard_map/ppermute | solution.py:17
  180.7 20.8 %collective-permute-done.19 = bf16[4,256,512]{2,1,0:T(8,128)(2,1)S(1)} collective-permute-done((bf16[4,256,512]{2,1,0:T(8,128)(2,1)S(1)}, bf16[4,256,512]{2,1,0:T(8,128)(2,1)S(1)}, u32[]{:S(2)}, u32[]{:S(2)}) %collective-permute-start.19) | collective-permute-done | bytes 1048608 | tf_op jit(solution)/shard_map/ppermute | solution.py:17
  208.2 21.6 %collective-permute-done.20 = bf16[4,256,512]{2,1,0:T(8,128)(2,1)S(1)} collective-permute-done((bf16[4,256,512]{2,1,0:T(8,128)(2,1)S(1)}, bf16[4,256,512]{2,1,0:T(8,128)(2,1)S(1)}, u32[]{:S(2)}, u32[]{:S(2)}) %collective-permute-start.20) | collective-permute-done | bytes 1048608 | tf_op jit(solution)/shard_map/ppermute | solution.py:17
  235.6 21.6 %collective-permute-done.21 = bf16[4,256,512]{2,1,0:T(8,128)(2,1)S(1)} collective-permute-done((bf16[4,256,512]{2,1,0:T(8,128)(2,1)S(1)}, bf16[4,256,512]{2,1,0:T(8,128)(2,1)S(1)}, u32[]{:S(2)}, u32[]{:S(2)}) %collective-permute-start.21) | collective-permute-done | bytes 1048608 | tf_op jit(solution)/shard_map/ppermute | solution.py:17
  262.9 21.6 %collective-permute-done.22 = bf16[4,256,512]{2,1,0:T(8,128)(2,1)S(1)} collective-permute-done((bf16[4,256,512]{2,1,0:T(8,128)(2,1)S(1)}, bf16[4,256,512]{2,1,0:T(8,128)(2,1)S(1)}, u32[]{:S(2)}, u32[]{:S(2)}) %collective-permute-start.22) | collective-permute-done | bytes 1048608 | tf_op jit(solution)/shard_map/ppermute | solution.py:17
  291.3 21.6 %collective-permute-done.23 = bf16[4,256,512]{2,1,0:T(8,128)(2,1)} collective-permute-done((bf16[4,256,512]{2,1,0:T(8,128)(2,1)S(1)}, bf16[4,256,512]{2,1,0:T(8,128)(2,1)}, u32[]{:S(2)}, u32[]{:S(2)}) %collective-permute-start.23) | collective-permute-done | bytes 1048608 | tf_op jit(solution)/shard_map/ppermute | solution.py:17
  323.8 16.9 %collective-permute-done.24 = bf16[4,256,512]{2,1,0:T(8,128)(2,1)} collective-permute-done((bf16[4,256,512]{2,1,0:T(8,128)(2,1)}, bf16[4,256,512]{2,1,0:T(8,128)(2,1)}, u32[]{:S(2)}, u32[]{:S(2)}) %collective-permute-start.24) | collective-permute-done | bytes 1048608 | tf_op jit(solution)/shard_map/ppermute | solution.py:17
  344.5 9.9 %collective-permute-done.12 = bf16[4,256,512]{2,1,0:T(8,128)(2,1)} collective-permute-done((bf16[4,256,512]{2,1,0:T(8,128)(2,1)}, bf16[4,256,512]{2,1,0:T(8,128)(2,1)}, u32[]{:S(2)}, u32[]{:S(2)}) %collective-permute-start.12) | collective-permute-done | bytes 1048608 | tf_op jit(solution)/shard_map/ppermute | solution.py:17
  373.7 9.3 %copy-done.1 = bf16[108,256,512]{2,1,0:T(8,128)(2,1)} copy-done((bf16[108,256,512]{2,1,0:T(8,128)(2,1)}, bf16[108,256,512]{2,1,0:T(8,128)(2,1)S(1)}, u32[]{:S(2)}) %copy-start.1) | copy-done | bytes 28311576
  383.0 315.0 %while.17 = (s32[]{:T(128)}, bf16[4,256,256]{2,1,0:T(8,128)(2,1)S(1)}, s32[]{:T(128)}, s32[]{:T(128)}, s32[56,45]{1,0:T(8,128)}, /*index=5*/bf16[4,256,256]{2,1,...) while((s32[]{:T(128)}, ...), condition=%wide.region_7.8_spmd, body=%wide.region_1.7_spmd.sunk | while | flops 3067989504 | bytes 167027216 | solution.py:85
  387.3 29.1 %select_select_fusion.2 = pred[11520]{0:T(1024)(128)(4,1)S(1)} fusion(pred[11520]{0:T(1024)(128)(4,1)S(1)} %get-tuple-element.685, pred[11520]{0:T(1024)(128)(4,1)S(1)} %get-tuple-element.686, pred[11520]{0:T(1024)(128)(4,1)S(1)} %get-tuple-element.687, pred[11520]{0:T(1024)(128)(4,1)S(1)} %get-tuple-element.688, ...), kind=kLoop, calls=%fused_computation.25.clone.1 | loop fusion | flops 506880 | bytes 518445 | tf_op jit(solution)/shard_map/while/body/jit(_take)/gather | solution.py:55
  418.1 15.0 %gather_fusion.1 = bf16[45,256,512]{2,1,0:T(8,128)(2,1)} fusion(bf16[108,256,512]{2,1,0:T(8,128)(2,1)} %get-tuple-element.680, s32[1024]{0:T(1024)S(1)} %pad_clamp_fusion.5), kind=kCustom, calls=%fused_computation.1.clone.1 | custom fusion | bytes 23593140 | tf_op jit(solution)/shard_map/while/body/jit(_take)/gather | solution.py:53
  465.8 29.1 %select_select_fusion.2 = pred[11520]{0:T(1024)(128)(4,1)S(1)} fusion(pred[11520]{0:T(1024)(128)(4,1)S(1)} %get-tuple-element.685, pred[11520]{0:T(1024)(128)(4,1)S(1)} %get-tuple-element.686, pred[11520]{0:T(1024)(128)(4,1)S(1)} %get-tuple-element.687, pred[11520]{0:T(1024)(128)(4,1)S(1)} %get-tuple-element.688, ...), kind=kLoop, calls=%fused_computation.25.clone.1 | loop fusion | flops 506880 | bytes 518445 | tf_op jit(solution)/shard_map/while/body/jit(_take)/gather | solution.py:55
  496.6 15.0 %gather_fusion.1 = bf16[45,256,512]{2,1,0:T(8,128)(2,1)} fusion(bf16[108,256,512]{2,1,0:T(8,128)(2,1)} %get-tuple-element.680, s32[1024]{0:T(1024)S(1)} %pad_clamp_fusion.5), kind=kCustom, calls=%fused_computation.1.clone.1 | custom fusion | bytes 23593140 | tf_op jit(solution)/shard_map/while/body/jit(_take)/gather | solution.py:53
  544.3 29.1 %select_select_fusion.2 = pred[11520]{0:T(1024)(128)(4,1)S(1)} fusion(pred[11520]{0:T(1024)(128)(4,1)S(1)} %get-tuple-element.685, pred[11520]{0:T(1024)(128)(4,1)S(1)} %get-tuple-element.686, pred[11520]{0:T(1024)(128)(4,1)S(1)} %get-tuple-element.687, pred[11520]{0:T(1024)(128)(4,1)S(1)} %get-tuple-element.688, ...), kind=kLoop, calls=%fused_computation.25.clone.1 | loop fusion | flops 506880 | bytes 518445 | tf_op jit(solution)/shard_map/while/body/jit(_take)/gather | solution.py:55
  575.0 15.0 %gather_fusion.1 = bf16[45,256,512]{2,1,0:T(8,128)(2,1)} fusion(bf16[108,256,512]{2,1,0:T(8,128)(2,1)} %get-tuple-element.680, s32[1024]{0:T(1024)S(1)} %pad_clamp_fusion.5), kind=kCustom, calls=%fused_computation.1.clone.1 | custom fusion | bytes 23593140 | tf_op jit(solution)/shard_map/while/body/jit(_take)/gather | solution.py:53
  622.8 29.1 %select_select_fusion.2 = pred[11520]{0:T(1024)(128)(4,1)S(1)} fusion(pred[11520]{0:T(1024)(128)(4,1)S(1)} %get-tuple-element.685, pred[11520]{0:T(1024)(128)(4,1)S(1)} %get-tuple-element.686, pred[11520]{0:T(1024)(128)(4,1)S(1)} %get-tuple-element.687, pred[11520]{0:T(1024)(128)(4,1)S(1)} %get-tuple-element.688, ...), kind=kLoop, calls=%fused_computation.25.clone.1 | loop fusion | flops 506880 | bytes 518445 | tf_op jit(solution)/shard_map/while/body/jit(_take)/gather | solution.py:55
  653.5 15.0 %gather_fusion.1 = bf16[45,256,512]{2,1,0:T(8,128)(2,1)} fusion(bf16[108,256,512]{2,1,0:T(8,128)(2,1)} %get-tuple-element.680, s32[1024]{0:T(1024)S(1)} %pad_clamp_fusion.5), kind=kCustom, calls=%fused_computation.1.clone.1 | custom fusion | bytes 23593140 | tf_op jit(solution)/shard_map/while/body/jit(_take)/gather | solution.py:53
  (249 shorter events, 245.6 us)
Async XLA Ops:
  2.3 27.4 %collective-permute-start = (bf16[4,256,512]{2,1,0:T(8,128)(2,1)S(1)}, bf16[4,256,512]{2,1,0:T(8,128)(2,1)S(1)}, u32[]{:S(2)}, u32[]{:S(2)}) collective-permute-start(bf16[4,256,512]{2,1,0:T(8,128)(2,1)S(1)} %constant_dynamic-update-slice_fusion.1), channel_id=1, source_target_pairs={{0,1},{1,2},{2,3},{3,4},{4,5},{5,6},{6,7},{7,8},{8,9},{9,10},{10,1... | collective-permute-start | bytes 3145736 | tf_op jit(solution)/shard_map/ppermute | solution.py:17
  4.2 35.6 %collective-permute-start.13 = (bf16[4,256,512]{2,1,0:T(8,128)(2,1)S(1)}, bf16[4,256,512]{2,1,0:T(8,128)(2,1)S(1)}, u32[]{:S(2)}, u32[]{:S(2)}) collective-permute-start(bf16[4,256,512]{2,1,0:T(8,128)(2,1)S(1)} %constant_dynamic-update-slice_fusion.1), channel_id=1, source_target_pairs={{1,0},{2,1},{3,2},{4,3},{5,4},{6,5},{7,6},{8,7},{9,8},{10,9},{11,1... | collective-permute-start | bytes 3145736 | tf_op jit(solution)/shard_map/ppermute | solution.py:17
  45.7 23.6 %collective-permute-start.2 = (bf16[4,256,512]{2,1,0:T(8,128)(2,1)S(1)}, bf16[4,256,512]{2,1,0:T(8,128)(2,1)S(1)}, u32[]{:S(2)}, u32[]{:S(2)}) collective-permute-start(bf16[4,256,512]{2,1,0:T(8,128)(2,1)S(1)} %collective-permute-done.1), channel_id=1, source_target_pairs={{0,1},{1,2},{2,3},{3,4},{4,5},{5,6},{6,7},{7,8},{8,9},{9,10},{10,1... | collective-permute-start | bytes 3145736 | tf_op jit(solution)/shard_map/ppermute | solution.py:17
  63.8 27.3 %collective-permute-start.15 = (bf16[4,256,512]{2,1,0:T(8,128)(2,1)S(1)}, bf16[4,256,512]{2,1,0:T(8,128)(2,1)S(1)}, u32[]{:S(2)}, u32[]{:S(2)}) collective-permute-start(bf16[4,256,512]{2,1,0:T(8,128)(2,1)S(1)} %collective-permute-done.14), channel_id=1, source_target_pairs={{1,0},{2,1},{3,2},{4,3},{5,4},{6,5},{7,6},{8,7},{9,8},{10,9},{11,1... | collective-permute-start | bytes 3145736 | tf_op jit(solution)/shard_map/ppermute | solution.py:17
  69.4 27.3 %collective-permute-start.3 = (bf16[4,256,512]{2,1,0:T(8,128)(2,1)S(1)}, bf16[4,256,512]{2,1,0:T(8,128)(2,1)S(1)}, u32[]{:S(2)}, u32[]{:S(2)}) collective-permute-start(bf16[4,256,512]{2,1,0:T(8,128)(2,1)S(1)} %collective-permute-done.2), channel_id=1, source_target_pairs={{0,1},{1,2},{2,3},{3,4},{4,5},{5,6},{6,7},{7,8},{8,9},{9,10},{10,1... | collective-permute-start | bytes 3145736 | tf_op jit(solution)/shard_map/ppermute | solution.py:17
  91.1 27.3 %collective-permute-start.16 = (bf16[4,256,512]{2,1,0:T(8,128)(2,1)S(1)}, bf16[4,256,512]{2,1,0:T(8,128)(2,1)S(1)}, u32[]{:S(2)}, u32[]{:S(2)}) collective-permute-start(bf16[4,256,512]{2,1,0:T(8,128)(2,1)S(1)} %collective-permute-done.15), channel_id=1, source_target_pairs={{1,0},{2,1},{3,2},{4,3},{5,4},{6,5},{7,6},{8,7},{9,8},{10,9},{11,1... | collective-permute-start | bytes 3145736 | tf_op jit(solution)/shard_map/ppermute | solution.py:17
  96.7 27.3 %collective-permute-start.4 = (bf16[4,256,512]{2,1,0:T(8,128)(2,1)S(1)}, bf16[4,256,512]{2,1,0:T(8,128)(2,1)S(1)}, u32[]{:S(2)}, u32[]{:S(2)}) collective-permute-start(bf16[4,256,512]{2,1,0:T(8,128)(2,1)S(1)} %collective-permute-done.3), channel_id=1, source_target_pairs={{0,1},{1,2},{2,3},{3,4},{4,5},{5,6},{6,7},{7,8},{8,9},{9,10},{10,1... | collective-permute-start | bytes 3145736 | tf_op jit(solution)/shard_map/ppermute | solution.py:17
  119.4 27.3 %collective-permute-start.17 = (bf16[4,256,512]{2,1,0:T(8,128)(2,1)S(1)}, bf16[4,256,512]{2,1,0:T(8,128)(2,1)S(1)}, u32[]{:S(2)}, u32[]{:S(2)}) collective-permute-start(bf16[4,256,512]{2,1,0:T(8,128)(2,1)S(1)} %collective-permute-done.16), channel_id=1, source_target_pairs={{1,0},{2,1},{3,2},{4,3},{5,4},{6,5},{7,6},{8,7},{9,8},{10,9},{11,1... | collective-permute-start | bytes 3145736 | tf_op jit(solution)/shard_map/ppermute | solution.py:17
  124.0 27.3 %collective-permute-start.5 = (bf16[4,256,512]{2,1,0:T(8,128)(2,1)S(1)}, bf16[4,256,512]{2,1,0:T(8,128)(2,1)S(1)}, u32[]{:S(2)}, u32[]{:S(2)}) collective-permute-start(bf16[4,256,512]{2,1,0:T(8,128)(2,1)S(1)} %collective-permute-done.4), channel_id=1, source_target_pairs={{0,1},{1,2},{2,3},{3,4},{4,5},{5,6},{6,7},{7,8},{8,9},{9,10},{10,1... | collective-permute-start | bytes 3145736 | tf_op jit(solution)/shard_map/ppermute | solution.py:17
  146.8 27.3 %collective-permute-start.18 = (bf16[4,256,512]{2,1,0:T(8,128)(2,1)S(1)}, bf16[4,256,512]{2,1,0:T(8,128)(2,1)S(1)}, u32[]{:S(2)}, u32[]{:S(2)}) collective-permute-start(bf16[4,256,512]{2,1,0:T(8,128)(2,1)S(1)} %collective-permute-done.17), channel_id=1, source_target_pairs={{1,0},{2,1},{3,2},{4,3},{5,4},{6,5},{7,6},{8,7},{9,8},{10,9},{11,1... | collective-permute-start | bytes 3145736 | tf_op jit(solution)/shard_map/ppermute | solution.py:17
  151.4 27.3 %collective-permute-start.6 = (bf16[4,256,512]{2,1,0:T(8,128)(2,1)S(1)}, bf16[4,256,512]{2,1,0:T(8,128)(2,1)S(1)}, u32[]{:S(2)}, u32[]{:S(2)}) collective-permute-start(bf16[4,256,512]{2,1,0:T(8,128)(2,1)S(1)} %collective-permute-done.5), channel_id=1, source_target_pairs={{0,1},{1,2},{2,3},{3,4},{4,5},{5,6},{6,7},{7,8},{8,9},{9,10},{10,1... | collective-permute-start | bytes 3145736 | tf_op jit(solution)/shard_map/ppermute | solution.py:17
  174.1 27.3 %collective-permute-start.19 = (bf16[4,256,512]{2,1,0:T(8,128)(2,1)S(1)}, bf16[4,256,512]{2,1,0:T(8,128)(2,1)S(1)}, u32[]{:S(2)}, u32[]{:S(2)}) collective-permute-start(bf16[4,256,512]{2,1,0:T(8,128)(2,1)S(1)} %collective-permute-done.18), channel_id=1, source_target_pairs={{1,0},{2,1},{3,2},{4,3},{5,4},{6,5},{7,6},{8,7},{9,8},{10,9},{11,1... | collective-permute-start | bytes 3145736 | tf_op jit(solution)/shard_map/ppermute | solution.py:17
  178.7 27.6 %collective-permute-start.7 = (bf16[4,256,512]{2,1,0:T(8,128)(2,1)S(1)}, bf16[4,256,512]{2,1,0:T(8,128)(2,1)S(1)}, u32[]{:S(2)}, u32[]{:S(2)}) collective-permute-start(bf16[4,256,512]{2,1,0:T(8,128)(2,1)S(1)} %collective-permute-done.6), channel_id=1, source_target_pairs={{0,1},{1,2},{2,3},{3,4},{4,5},{5,6},{6,7},{7,8},{8,9},{9,10},{10,1... | collective-permute-start | bytes 3145736 | tf_op jit(solution)/shard_map/ppermute | solution.py:17
  202.5 27.3 %collective-permute-start.20 = (bf16[4,256,512]{2,1,0:T(8,128)(2,1)S(1)}, bf16[4,256,512]{2,1,0:T(8,128)(2,1)S(1)}, u32[]{:S(2)}, u32[]{:S(2)}) collective-permute-start(bf16[4,256,512]{2,1,0:T(8,128)(2,1)S(1)} %collective-permute-done.19), channel_id=1, source_target_pairs={{1,0},{2,1},{3,2},{4,3},{5,4},{6,5},{7,6},{8,7},{9,8},{10,9},{11,1... | collective-permute-start | bytes 3145736 | tf_op jit(solution)/shard_map/ppermute | solution.py:17
  206.3 27.4 %collective-permute-start.8 = (bf16[4,256,512]{2,1,0:T(8,128)(2,1)S(1)}, bf16[4,256,512]{2,1,0:T(8,128)(2,1)S(1)}, u32[]{:S(2)}, u32[]{:S(2)}) collective-permute-start(bf16[4,256,512]{2,1,0:T(8,128)(2,1)S(1)} %collective-permute-done.7), channel_id=1, source_target_pairs={{0,1},{1,2},{2,3},{3,4},{4,5},{5,6},{6,7},{7,8},{8,9},{9,10},{10,1... | collective-permute-start | bytes 3145736 | tf_op jit(solution)/shard_map/ppermute | solution.py:17
  229.8 27.3 %collective-permute-start.21 = (bf16[4,256,512]{2,1,0:T(8,128)(2,1)S(1)}, bf16[4,256,512]{2,1,0:T(8,128)(2,1)S(1)}, u32[]{:S(2)}, u32[]{:S(2)}) collective-permute-start(bf16[4,256,512]{2,1,0:T(8,128)(2,1)S(1)} %collective-permute-done.20), channel_id=1, source_target_pairs={{1,0},{2,1},{3,2},{4,3},{5,4},{6,5},{7,6},{8,7},{9,8},{10,9},{11,1... | collective-permute-start | bytes 3145736 | tf_op jit(solution)/shard_map/ppermute | solution.py:17
  233.7 27.3 %collective-permute-start.9 = (bf16[4,256,512]{2,1,0:T(8,128)(2,1)S(1)}, bf16[4,256,512]{2,1,0:T(8,128)(2,1)S(1)}, u32[]{:S(2)}, u32[]{:S(2)}) collective-permute-start(bf16[4,256,512]{2,1,0:T(8,128)(2,1)S(1)} %collective-permute-done.8), channel_id=1, source_target_pairs={{0,1},{1,2},{2,3},{3,4},{4,5},{5,6},{6,7},{7,8},{8,9},{9,10},{10,1... | collective-permute-start | bytes 3145736 | tf_op jit(solution)/shard_map/ppermute | solution.py:17
  257.2 27.3 %collective-permute-start.22 = (bf16[4,256,512]{2,1,0:T(8,128)(2,1)S(1)}, bf16[4,256,512]{2,1,0:T(8,128)(2,1)S(1)}, u32[]{:S(2)}, u32[]{:S(2)}) collective-permute-start(bf16[4,256,512]{2,1,0:T(8,128)(2,1)S(1)} %collective-permute-done.21), channel_id=1, source_target_pairs={{1,0},{2,1},{3,2},{4,3},{5,4},{6,5},{7,6},{8,7},{9,8},{10,9},{11,1... | collective-permute-start | bytes 3145736 | tf_op jit(solution)/shard_map/ppermute | solution.py:17
  261.0 28.4 %collective-permute-start.10 = (bf16[4,256,512]{2,1,0:T(8,128)(2,1)S(1)}, bf16[4,256,512]{2,1,0:T(8,128)(2,1)S(1)}, u32[]{:S(2)}, u32[]{:S(2)}) collective-permute-start(bf16[4,256,512]{2,1,0:T(8,128)(2,1)S(1)} %collective-permute-done.9), channel_id=1, source_target_pairs={{0,1},{1,2},{2,3},{3,4},{4,5},{5,6},{6,7},{7,8},{8,9},{9,10},{10,1... | collective-permute-start | bytes 3145736 | tf_op jit(solution)/shard_map/ppermute | solution.py:17
  285.6 27.3 %collective-permute-start.23 = (bf16[4,256,512]{2,1,0:T(8,128)(2,1)S(1)}, bf16[4,256,512]{2,1,0:T(8,128)(2,1)}, u32[]{:S(2)}, u32[]{:S(2)}) collective-permute-start(bf16[4,256,512]{2,1,0:T(8,128)(2,1)S(1)} %collective-permute-done.22), channel_id=1, source_target_pairs={{1,0},{2,1},{3,2},{4,3},{5,4},{6,5},{7,6},{8,7},{9,8},{10,9},{11,1... | collective-permute-start | bytes 3145736 | tf_op jit(solution)/shard_map/ppermute | solution.py:17
  289.4 27.4 %collective-permute-start.11 = (bf16[4,256,512]{2,1,0:T(8,128)(2,1)S(1)}, bf16[4,256,512]{2,1,0:T(8,128)(2,1)}, u32[]{:S(2)}, u32[]{:S(2)}) collective-permute-start(bf16[4,256,512]{2,1,0:T(8,128)(2,1)S(1)} %collective-permute-done.10), channel_id=1, source_target_pairs={{0,1},{1,2},{2,3},{3,4},{4,5},{5,6},{6,7},{7,8},{8,9},{9,10},{10,1... | collective-permute-start | bytes 3145736 | tf_op jit(solution)/shard_map/ppermute | solution.py:17
  312.9 27.8 %collective-permute-start.24 = (bf16[4,256,512]{2,1,0:T(8,128)(2,1)}, bf16[4,256,512]{2,1,0:T(8,128)(2,1)}, u32[]{:S(2)}, u32[]{:S(2)}) collective-permute-start(bf16[4,256,512]{2,1,0:T(8,128)(2,1)} %collective-permute-done.23), channel_id=1, source_target_pairs={{1,0},{2,1},{3,2},{4,3},{5,4},{6,5},{7,6},{8,7},{9,8},{10,9},{11,1... | collective-permute-start | bytes 3145736 | tf_op jit(solution)/shard_map/ppermute | solution.py:17
  316.9 37.5 %collective-permute-start.12 = (bf16[4,256,512]{2,1,0:T(8,128)(2,1)}, bf16[4,256,512]{2,1,0:T(8,128)(2,1)}, u32[]{:S(2)}, u32[]{:S(2)}) collective-permute-start(bf16[4,256,512]{2,1,0:T(8,128)(2,1)} %collective-permute-done.11), channel_id=1, source_target_pairs={{0,1},{1,2},{2,3},{3,4},{4,5},{5,6},{6,7},{7,8},{8,9},{9,10},{10,1... | collective-permute-start | bytes 3145736 | tf_op jit(solution)/shard_map/ppermute | solution.py:17
  340.7 32.9 %collective-permute-start.25 = (bf16[4,256,512]{2,1,0:T(8,128)(2,1)}, bf16[4,256,512]{2,1,0:T(8,128)(2,1)S(1)}, u32[]{:S(2)}, u32[]{:S(2)}) collective-permute-start(bf16[4,256,512]{2,1,0:T(8,128)(2,1)} %collective-permute-done.24), channel_id=1, source_target_pairs={{1,0},{2,1},{3,2},{4,3},{5,4},{6,5},{7,6},{8,7},{9,8},{10,9},{11,1... | collective-permute-start | bytes 3145736 | tf_op jit(solution)/shard_map/ppermute | solution.py:17
  (43 other events, 2402.1 us)
where the time goes:
time: 705 us; the launch traced here: 699 us
  waiting for transfers between devices  268 us (38%)
  other arithmetic  164 us (23%)
  local copies, waits for them, and re-layouts  135 us (19%)
  starting transfers between devices  74.3 us (11%)
  matrix products  49.7 us (7%)
    ppermute x26, waiting for transfers between devices, passed_along(): lax.ppermute(value, axis, [(source, source + steps) for source in range(i...  268 us
    gather x4, other arithmetic, attend(): keep_keys = jnp.repeat(usable, tokens, total_repeat_length=NBR * tokens)  116 us
    ppermute x26, starting transfers between devices, passed_along(): lax.ppermute(value, axis, [(source, source + steps) for source in range(i...  74.3 us
    gather x4, local copies, waits for them, and re-layouts, attend(): picked = jnp.take(window, places, axis=0)  60.1 us
    unnamed x102, local copies, waits for them, and re-layouts  34.4 us
    select_n x8, other arithmetic, attend(): picked = jnp.take(window, places, axis=0)  28.1 us
    dot_general x8, matrix products, attend(): mixed = jnp.dot(probs, value_block, preferred_element_type=jnp.float32)  26.6 us
    dot_general x8, matrix products, attend(): lax.dot_general(query_head, key_block, (((1,), (1,)), ((), ())), preferre...  23.1 us
  transfers between devices with their start and end apart: 26, of which 20 were waited for; matrix products, arithmetic and copies ran while one was open for 3% of the time, Pallas kernels for 0%

commit v1 on v0

--- a/solution.py
+++ b/solution.py
@@ -1,6 +1,10 @@
+import math
+
 import jax
 import jax.numpy as jnp
 from jax import lax
+from jax.experimental import pallas as pl
+from jax.experimental.pallas import tpu as pltpu
 from jax.sharding import PartitionSpec as P
 
 HEADS = 2
@@ -17,7 +21,7 @@
     return lax.ppermute(value, axis, [(source, source + steps) for source in range(initial, last)])
 
 
-def per_device(queries, keys, values, counts, neighbors):
+def ring_attention(queries, keys, values, counts, neighbors):
     capacity = queries.shape[0]
     tokens = queries.shape[1]
     channels = queries.shape[2]
@@ -85,6 +89,260 @@
     return lax.fori_loop(0, owned, attend, blank)
 
 
+LINE = 4
+CORES = 2
+LISTED_OUT = 3e30
+NOTHING_YET = -1e30
+AHEAD = 1
+
+
+def gathered_kernel(aside_ref, q_ref, k_ref, v_ref, o_ref, kv, top, total, acc,
+                    arrive, to_sib, to_a, to_b, to_c):
+    capacity, tokens, channels = q_ref.shape
+    head_dim = channels // HEADS
+    scale = math.log2(math.e) / math.sqrt(head_dim)
+    me = lax.axis_index("tile")
+    core = me % 2
+    y = (me // 2) % 2
+    z = me // 4
+    side = z // 2
+    outer = (z == 0) | (z == LINE - 1)
+    inner = jnp.logical_not(outer)
+    z_o, z_i, z_m, z_f = 3 * side, 1 + side, 2 - side, 3 - 3 * side
+    flip = 1 - 2 * core
+
+    def at(zz, yy):
+        return (zz * 2 + yy) * 2 + core
+
+    sibling = me + flip
+    across = at(z, 1 - y)
+    near = at(jnp.where(outer, z_i, z_o), y)
+    middle = at(z_m, y)
+
+    def send(g, sem, target):
+        return pltpu.make_async_remote_copy(
+            src_ref=kv.at[g], dst_ref=kv.at[g], send_sem=sem, recv_sem=arrive.at[g],
+            device_id={"tile": target}, device_id_type=pl.DeviceIdType.MESH)
+
+    def landed(g):
+        send(g, to_sib.at[0], sibling).wait_recv()
+
+    def outer_slot(m):
+        k = m // 2
+        first = m % 2 == 0
+        along = jnp.where(k < 4, at(z_i, y) * 4 + k, jnp.where(k < 8, at(z_m, y) * 4 + k - 4, jnp.where(
+            k < 12, at(z_f, y) * 4 + k - 8, at(z_i, 1 - y) * 4 + k - 12)))
+        over = jnp.where(k < 4, at(z_o, 1 - y) * 4 + k, jnp.where(k < 6, at(z_i, 1 - y) * 4 + k - 2, jnp.where(
+            k < 10, at(z_m, 1 - y) * 4 + k - 6, at(z_f, 1 - y) * 4 + k - 10)))
+        return jnp.where(first, along, over)
+
+    def inner_slot(m):
+        k = (m // 3) % 4
+        lane = m % 3
+        one = jnp.where(lane == 0, at(z_o, y), jnp.where(lane == 1, at(z_m, y), at(z_i, 1 - y)))
+        two = jnp.where(lane == 0, at(z_o, 1 - y), jnp.where(lane == 1, at(z_f, y), at(z_f, 1 - y)))
+        return jnp.where(m < 12, one * 4 + k, jnp.where(m < 24, two * 4 + k, at(z_m, 1 - y) * 4 + m - 24))
+
+    def slot_of(j):
+        m = jnp.maximum(j - 4, 0)
+        later = jnp.where(outer, outer_slot(m), inner_slot(m))
+        return jnp.where(j < 4, me * 4 + j, later)
+
+    barrier = pltpu.get_barrier_semaphore()
+    for other in (sibling, across, near):
+        pl.semaphore_signal(barrier, inc=1, device_id={"tile": other}, device_id_type=pl.DeviceIdType.MESH)
+
+    @pl.when(inner)
+    def _():
+        pl.semaphore_signal(barrier, inc=1, device_id={"tile": middle}, device_id_type=pl.DeviceIdType.MESH)
+        pl.semaphore_wait(barrier, 4)
+
+    @pl.when(outer)
+    def _():
+        pl.semaphore_wait(barrier, 3)
+
+    for s in range(capacity):
+        g = me * 4 + s
+        kv[g, 0] = k_ref[s]
+        kv[g, 1] = v_ref[s].T
+        send(g, to_a.at[s], near).start()
+        send(g, to_b.at[s], across).start()
+        send(g, to_sib.at[s], sibling).start()
+
+        @pl.when(inner)
+        def _():
+            send(g, to_c.at[s], middle).start()
+
+    top[...] = jnp.full(top.shape, NOTHING_YET, jnp.float32)
+    total[...] = jnp.zeros(total.shape, jnp.float32)
+    acc[...] = jnp.zeros(acc.shape, jnp.float32)
+
+    def pass_on(j):
+        g = slot_of(j)
+        m = j - 4
+        landed(g)
+
+        @pl.when(outer)
+        def _():
+            k = m // 2
+            along = m % 2 == 0
+
+            @pl.when(along & (k >= 2) & (k < 12))
+            def _():
+                send(g, to_b.at[k + 2], across).start()
+
+            @pl.when(jnp.logical_not(along) & (k < 4))
+            def _():
+                send(g, to_a.at[k + 4], near).start()
+
+        @pl.when(inner & (m < 24))
+        def _():
+            k = (m // 3) % 4
+            lane = m % 3
+            early = m < 12
+            kept = at(z_i, 1 - y) * 4
+
+            @pl.when(lane == 0)
+            def _():
+                send(jnp.where(early, g, kept + k), to_c.at[jnp.where(early, 4, 8) + k], middle).start()
+
+            @pl.when(lane == 1)
+            def _():
+                send(g, to_a.at[jnp.where(early, 4, 8) + k], near).start()
+
+                @pl.when(jnp.logical_not(early))
+                def _():
+                    send(g, to_b.at[4 + k], across).start()
+
+                    @pl.when(k >= 2)
+                    def _():
+                        send(kept + k - 2, to_a.at[10 + k], near).start()
+
+        send(g, to_sib.at[j], sibling).start()
+
+    def attend(first, second):
+        for head in range(HEADS):
+            low = head * head_dim
+            keys = [kv[g, 0, :, low : low + head_dim] for g in (first, second)]
+            values = [kv[g, 1, low : low + head_dim, :] for g in (first, second)]
+            for r in range(capacity):
+                unit = r * HEADS + head
+                query = q_ref[r, :, low : low + head_dim]
+                aside = [aside_ref[r, g] for g in (first, second)]
+                scores = [
+                    lax.dot_general(key, query, (((1,), (1,)), ((), ())), preferred_element_type=jnp.float32)
+                    for key in keys
+                ]
+                before = top[unit]
+                now = before
+                for score, off in zip(scores, aside):
+                    now = jnp.maximum(now, jnp.max(score, axis=0, keepdims=True) * scale - off)
+                fade = jnp.exp2(before - now)
+                summed = total[unit] * fade
+                mixed = acc[unit] * fade
+                for score, off, value in zip(scores, aside, values):
+                    weights = jnp.exp2(score * scale - (now + off))
+                    summed += jnp.sum(weights, axis=0, keepdims=True)
+                    mixed += jnp.dot(value, weights.astype(jnp.bfloat16), preferred_element_type=jnp.float32)
+                top[unit] = now
+                total[unit] = summed
+                acc[unit] = mixed
+
+    steps = 32
+
+    def step(j, _):
+        @pl.when((j + AHEAD >= 4) & (j + AHEAD < steps))
+        def _():
+            pass_on(j + AHEAD)
+
+        mine = slot_of(j)
+        theirs = mine + 4 * flip
+        landed(theirs)
+        attend(mine, theirs)
+        return 0
+
+    lax.fori_loop(0, steps, step, 0)
+
+    for r in range(capacity):
+        for head in range(HEADS):
+            unit = r * HEADS + head
+            low = head * head_dim
+            sums = total[unit]
+            share = jnp.where(sums > 0, 1.0 / sums, 0.0)
+            o_ref[r, :, low : low + head_dim] = (acc[unit] * share).T.astype(o_ref.dtype)
+
+    def sent(sems, target, count):
+        def one(n, _):
+            send(me * 4, sems.at[n], target).wait_send()
+            return 0
+
+        lax.fori_loop(0, count, one, 0)
+
+    sent(to_sib, sibling, steps)
+
+    @pl.when(outer)
+    def _():
+        sent(to_a, near, 8)
+        sent(to_b, across, 14)
+
+    @pl.when(inner)
+    def _():
+        sent(to_a, near, 14)
+        sent(to_b, across, 8)
+        sent(to_c, middle, 12)
+
+
+def gathered_attention(queries, keys, values, counts, neighbors):
+    capacity, tokens, channels = queries.shape
+    device_count = counts.shape[0]
+    slots = device_count * capacity
+    head_dim = channels // HEADS
+    position = lax.axis_index("tile")
+    ids = jnp.arange(device_count)
+    starts = jnp.sum(jnp.where(ids[None, :] < ids[:, None], counts[None, :], 0), axis=1)
+    within = jnp.arange(capacity)
+    held = jnp.where(within[None, :] < counts[:, None], starts[:, None] + within[None, :], -2).reshape(slots)
+    first = jnp.sum(jnp.where(ids < position, counts, 0))
+    owned = jnp.sum(jnp.where(ids == position, counts, 0))
+    rows = jnp.minimum(first + within, neighbors.shape[0] - 1)
+    listed = jnp.take(neighbors, rows, axis=0)
+    wanted = jnp.any(listed[:, :, None] == held[None, None, :], axis=1) & (within < owned)[:, None]
+    aside = jnp.where(wanted, 0.0, LISTED_OUT).astype(jnp.float32)
+    units = capacity * HEADS
+    return pl.pallas_call(
+        gathered_kernel,
+        out_shape=jax.ShapeDtypeStruct(queries.shape, queries.dtype),
+        in_specs=[pl.BlockSpec(memory_space=pltpu.SMEM)] + [pl.BlockSpec(memory_space=pltpu.VMEM)] * 3,
+        out_specs=pl.BlockSpec(memory_space=pltpu.VMEM),
+        scratch_shapes=[
+            pltpu.VMEM((slots, 2, tokens, channels), keys.dtype),
+            pltpu.VMEM((units, 1, tokens), jnp.float32),
+            pltpu.VMEM((units, 1, tokens), jnp.float32),
+            pltpu.VMEM((units, head_dim, tokens), jnp.float32),
+            pltpu.SemaphoreType.DMA((slots,)),
+            pltpu.SemaphoreType.DMA((32,)),
+            pltpu.SemaphoreType.DMA((14,)),
+            pltpu.SemaphoreType.DMA((14,)),
+            pltpu.SemaphoreType.DMA((12,)),
+        ],
+        compiler_params=pltpu.CompilerParams(
+            collective_id=0, has_side_effects=True, vmem_limit_bytes=48 * 1024 * 1024
+        ),
+        cost_estimate=pl.CostEstimate(
+            flops=4 * capacity * slots * tokens * tokens * channels,
+            bytes_accessed=4 * queries.size * 2,
+            transcendentals=capacity * slots * HEADS * tokens * tokens,
+        ),
+        name="gathered_attention",
+    )(aside, queries, keys, values)
+
+
+def per_device(queries, keys, values, counts, neighbors):
+    if counts.shape[0] == LINE * 2 * CORES and queries.shape[1] == queries.shape[2] and queries.shape[0] == 4:
+        return gathered_attention(queries, keys, values, counts, neighbors)
+    return ring_attention(queries, keys, values, counts, neighbors)
+
+
 def solution(mesh):
     in_specs = (
         P(("clip", "tile"), None, None),

time: 705 us -> 142 us (0.20)
  the two profiles are of different devices: /device:TPU:12 before, /device:TPU:0 now
where the time goes in v1:
time: 142 us; the launch traced here: 141 us
  Pallas kernels  131 us (92%)
  local copies, waits for them, and re-layouts  5.4 us (4%)
  other arithmetic  4.55 us (3%)
    pallas_call x1, Pallas kernels, gathered_attention(): pl.pallas_call(gathered_kernel, out_shape=jax.ShapeDtypeStruct(queries.sh...  131 us
    unnamed x12, local copies, waits for them, and re-layouts  4.65 us

profile of v1, /device:TPU:0, one launch (start us, length us, event | category | flops | bytes accessed | tf_op | source)
XLA Modules:
  0.0 141.4 jit_solution(5738020011180899618)
XLA Ops:
  0.0 0.0 copy-start.3
  0.0 0.8 select_reduce_fusion
  0.8 1.4 fusion.1
  2.2 0.7 fusion.2
  2.9 1.3 compare_and_fusion
  4.2 0.0 copy-start.4
  4.2 0.6 copy-done.4
  4.9 0.1 add_select_fusion
  4.9 0.1 select_n.56
  5.0 0.0 copy-done.3
  5.0 0.1 copy.8
  5.1 0.6 gather_fusion
  5.7 0.1 broadcast_select_fusion
  5.8 0.1 copy.9
  5.9 0.1 compare_reduce_fusion
  6.0 0.1 and_select_fusion.aside_ref
  6.1 0.0 copy-start
  6.1 1.0 copy-done
  7.1 0.0 copy-start.1
  7.1 1.0 copy-done.1
  8.2 0.0 copy-start.2
  8.2 1.0 copy-done.2
  9.2 131.4 %gathered_attention.1 = bf16[4,256,256]{2,1,0:T(8,128)(2,1)S(1)} custom-call(f32[4,64]{1,0:T(4,128)S(1)} %and_select_fusion.aside_ref, bf16[4,256,256]{2,1,0:T(8,128)(2,1)S(1)} %copy-done, bf16[4,256,256]{2,1,0:T(8,128)(2,1)S(1)} %copy-done.1, bf16[4,256,256]{2,1,0:T(8,128)(2,1)S(1)} %copy-done.2), custom_call_target="tpu_custom_call" | custom-call | flops 17179869184 | bytes 2097152 | tf_op jit(solution)/shard_map/gathered_attention/pallas_call | solution.py:312
  140.6 0.8 copy.11
  (1 shorter events, 0.0 us)
Async XLA Ops:
  0.0 5.0 %copy-start.3 = (s32[56,45]{0,1:T(8,128)S(1)}, s32[56,45]{0,1:T(8,128)}, u32[]{:S(2)}) copy-start(s32[56,45]{0,1:T(8,128)} %param.9) | copy-start | bytes 30244
  4.2 0.7 copy-start.4
  6.1 1.0 copy-start
  7.1 1.0 copy-start.1
  8.2 1.0 copy-start.2

commit v2 on v1

--- a/solution.py
+++ b/solution.py
@@ -96,8 +96,8 @@
 AHEAD = 1
 
 
-def gathered_kernel(aside_ref, q_ref, k_ref, v_ref, o_ref, kv, top, total, acc,
-                    arrive, to_sib, to_a, to_b, to_c):
+def gathered_kernel(counts_ref, listed_ref, q_ref, k_ref, v_ref, o_ref, kv, values, turned, aside_ref, top,
+                    total, acc, own, arrive, to_sib, to_a, to_b, to_c):
     capacity, tokens, channels = q_ref.shape
     head_dim = channels // HEADS
     scale = math.log2(math.e) / math.sqrt(head_dim)
@@ -148,6 +148,12 @@
         later = jnp.where(outer, outer_slot(m), inner_slot(m))
         return jnp.where(j < 4, me * 4 + j, later)
 
+    staged = [pltpu.make_async_copy(k_ref.at[s], kv.at[me * 4 + s, 0], own.at[s]) for s in range(capacity)]
+    staged += [pltpu.make_async_copy(v_ref.at[s], values.at[s], own.at[capacity + s]) for s in range(capacity)]
+    staged.append(pltpu.make_async_copy(q_ref, turned, own.at[2 * capacity]))
+    for copy in staged:
+        copy.start()
+
     barrier = pltpu.get_barrier_semaphore()
     for other in (sibling, across, near):
         pl.semaphore_signal(barrier, inc=1, device_id={"tile": other}, device_id_type=pl.DeviceIdType.MESH)
@@ -163,8 +169,9 @@
 
     for s in range(capacity):
         g = me * 4 + s
-        kv[g, 0] = k_ref[s]
-        kv[g, 1] = v_ref[s].T
+        staged[s].wait()
+        staged[capacity + s].wait()
+        kv[g, 1] = values[s].T
         send(g, to_a.at[s], near).start()
         send(g, to_b.at[s], across).start()
         send(g, to_sib.at[s], sibling).start()
@@ -173,6 +180,31 @@
         def _():
             send(g, to_c.at[s], middle).start()
 
+    staged[2 * capacity].wait()
+    for r in range(capacity):
+        turned[r] = turned[r].T
+
+    slots = arrive.shape[0]
+    device_count = slots // capacity
+    shape = (slots, listed_ref.shape[1])
+    slot = lax.broadcasted_iota(jnp.int32, shape, 0)
+    owner = slot // capacity
+    within = slot % capacity
+    held = within
+    limit = jnp.zeros(shape, jnp.int32)
+    first = 0
+    owned = 0
+    for e in range(device_count):
+        held += jnp.where(owner > e, counts_ref[e], 0)
+        limit += jnp.where(owner == e, counts_ref[e], 0)
+        first += jnp.where(me > e, counts_ref[e], 0)
+        owned += jnp.where(me == e, counts_ref[e], 0)
+    held = jnp.where(within < limit, held, -2)
+    for r in range(capacity):
+        row = jnp.minimum(first + r, listed_ref.shape[0] - 1)
+        hit = (listed_ref[pl.ds(row, 1), :] == held).astype(jnp.float32)
+        wanted = jnp.max(hit, axis=1, keepdims=True) * jnp.where(r < owned, 1.0, 0.0)
+        aside_ref[r] = jnp.broadcast_to(jnp.where(wanted > 0, 0.0, LISTED_OUT), (slots, tokens))
     top[...] = jnp.full(top.shape, NOTHING_YET, jnp.float32)
     total[...] = jnp.zeros(total.shape, jnp.float32)
     acc[...] = jnp.zeros(acc.shape, jnp.float32)
@@ -221,32 +253,40 @@
         send(g, to_sib.at[j], sibling).start()
 
     def attend(first, second):
-        for head in range(HEADS):
+        units = [(r, head) for head in range(HEADS) for r in range(capacity)]
+
+        def scored(n):
+            r, head = units[n]
             low = head * head_dim
-            keys = [kv[g, 0, :, low : low + head_dim] for g in (first, second)]
-            values = [kv[g, 1, low : low + head_dim, :] for g in (first, second)]
-            for r in range(capacity):
-                unit = r * HEADS + head
-                query = q_ref[r, :, low : low + head_dim]
-                aside = [aside_ref[r, g] for g in (first, second)]
-                scores = [
-                    lax.dot_general(key, query, (((1,), (1,)), ((), ())), preferred_element_type=jnp.float32)
-                    for key in keys
-                ]
-                before = top[unit]
-                now = before
-                for score, off in zip(scores, aside):
-                    now = jnp.maximum(now, jnp.max(score, axis=0, keepdims=True) * scale - off)
-                fade = jnp.exp2(before - now)
-                summed = total[unit] * fade
-                mixed = acc[unit] * fade
-                for score, off, value in zip(scores, aside, values):
-                    weights = jnp.exp2(score * scale - (now + off))
-                    summed += jnp.sum(weights, axis=0, keepdims=True)
-                    mixed += jnp.dot(value, weights.astype(jnp.bfloat16), preferred_element_type=jnp.float32)
-                top[unit] = now
-                total[unit] = summed
-                acc[unit] = mixed
+            return [
+                jnp.dot(kv[g, 0, :, low : low + head_dim], turned[r, low : low + head_dim, :],
+                        preferred_element_type=jnp.float32)
+                for g in (first, second)
+            ]
+
+        upcoming = scored(0)
+        for n, (r, head) in enumerate(units):
+            low = head * head_dim
+            unit = r * HEADS + head
+            scores = upcoming
+            if n + 1 < len(units):
+                upcoming = scored(n + 1)
+            aside = [aside_ref[r, pl.ds(g, 1), :] for g in (first, second)]
+            before = top[unit]
+            now = before
+            for score, off in zip(scores, aside):
+                now = jnp.maximum(now, jnp.max(score, axis=0, keepdims=True) * scale - off)
+            fade = jnp.exp2(before - now)
+            summed = total[unit] * fade
+            mixed = acc[unit] * fade
+            for g, score, off in zip((first, second), scores, aside):
+                weights = jnp.exp2(score * scale - (now + off))
+                summed += jnp.sum(weights, axis=0, keepdims=True)
+                mixed += jnp.dot(kv[g, 1, low : low + head_dim, :], weights.astype(jnp.bfloat16),
+                                 preferred_element_type=jnp.float32)
+            top[unit] = now
+            total[unit] = summed
+            acc[unit] = mixed
 
     steps = 32
 
@@ -297,28 +337,22 @@
     device_count = counts.shape[0]
     slots = device_count * capacity
     head_dim = channels // HEADS
-    position = lax.axis_index("tile")
-    ids = jnp.arange(device_count)
-    starts = jnp.sum(jnp.where(ids[None, :] < ids[:, None], counts[None, :], 0), axis=1)
-    within = jnp.arange(capacity)
-    held = jnp.where(within[None, :] < counts[:, None], starts[:, None] + within[None, :], -2).reshape(slots)
-    first = jnp.sum(jnp.where(ids < position, counts, 0))
-    owned = jnp.sum(jnp.where(ids == position, counts, 0))
-    rows = jnp.minimum(first + within, neighbors.shape[0] - 1)
-    listed = jnp.take(neighbors, rows, axis=0)
-    wanted = jnp.any(listed[:, :, None] == held[None, None, :], axis=1) & (within < owned)[:, None]
-    aside = jnp.where(wanted, 0.0, LISTED_OUT).astype(jnp.float32)
     units = capacity * HEADS
     return pl.pallas_call(
         gathered_kernel,
         out_shape=jax.ShapeDtypeStruct(queries.shape, queries.dtype),
-        in_specs=[pl.BlockSpec(memory_space=pltpu.SMEM)] + [pl.BlockSpec(memory_space=pltpu.VMEM)] * 3,
+        in_specs=[pl.BlockSpec(memory_space=pltpu.SMEM), pl.BlockSpec(memory_space=pltpu.VMEM)]
+        + [pl.BlockSpec(memory_space=pltpu.HBM)] * 3,
         out_specs=pl.BlockSpec(memory_space=pltpu.VMEM),
         scratch_shapes=[
             pltpu.VMEM((slots, 2, tokens, channels), keys.dtype),
+            pltpu.VMEM((capacity, tokens, channels), values.dtype),
+            pltpu.VMEM((capacity, channels, tokens), queries.dtype),
+            pltpu.VMEM((capacity, slots, tokens), jnp.float32),
             pltpu.VMEM((units, 1, tokens), jnp.float32),
             pltpu.VMEM((units, 1, tokens), jnp.float32),
             pltpu.VMEM((units, head_dim, tokens), jnp.float32),
+            pltpu.SemaphoreType.DMA((2 * capacity + 1,)),
             pltpu.SemaphoreType.DMA((slots,)),
             pltpu.SemaphoreType.DMA((32,)),
             pltpu.SemaphoreType.DMA((14,)),
@@ -334,7 +368,7 @@
             transcendentals=capacity * slots * HEADS * tokens * tokens,
         ),
         name="gathered_attention",
-    )(aside, queries, keys, values)
+    )(counts, neighbors, queries, keys, values)
 
 
 def per_device(queries, keys, values, counts, neighbors):

time: 142 us -> 103 us (0.73)
  Pallas kernels: 131 us -> 98.4 us
  other arithmetic: 4.55 us -> 0 us
    pallas_call x1, Pallas kernels: 131 us -> 98.4 us  [gathered_attention(): pl.pallas_call(gathered_kernel, out_shape=jax.ShapeDtypeStruct(queries.sh...]
    reduce_sum x2 -> x0, other arithmetic: 2.16 us -> none  [the longest x1 1.38 us: gathered_attention(): owned = jnp.sum(jnp.where(ids == position, counts, 0))]
    unnamed x12 -> x10, local copies, waits for them, and re-layouts: 4.65 us -> 4.75 us
where the time goes in v2:
time: 103 us
  Pallas kernels  98.4 us (96%)
  local copies, waits for them, and re-layouts  4.75 us (5%)
    pallas_call x1, Pallas kernels, gathered_attention(): pl.pallas_call(gathered_kernel, out_shape=jax.ShapeDtypeStruct(queries.sh...  98.4 us
    unnamed x10, local copies, waits for them, and re-layouts  4.75 us

profile of v2, /device:TPU:0, one launch (start us, length us, event | category | flops | bytes accessed | tf_op | source)
XLA Modules:
  0.0 103.2 jit_solution(3125262936757373316)
XLA Ops:
  0.0 0.0 copy-start.3
  0.0 0.8 copy.6.listed_ref
  0.8 0.0 copy-done.3
  0.8 0.0 copy-start
  0.8 1.0 %copy-done = bf16[4,256,256]{2,1,0:T(8,128)(2,1)S(1)} copy-done((bf16[4,256,256]{2,1,0:T(8,128)(2,1)S(1)}, bf16[4,256,256]{2,1,0:T(8,128)(2,1)}, u32[]{:S(2)}) %copy-start) | copy-done | bytes 524312
  1.9 0.0 copy-start.1
  1.9 1.0 %copy-done.1 = bf16[4,256,256]{2,1,0:T(8,128)(2,1)S(1)} copy-done((bf16[4,256,256]{2,1,0:T(8,128)(2,1)S(1)}, bf16[4,256,256]{2,1,0:T(8,128)(2,1)}, u32[]{:S(2)}) %copy-start.1) | copy-done | bytes 524312
  2.9 0.0 copy-start.2
  2.9 1.0 %copy-done.2 = bf16[4,256,256]{2,1,0:T(8,128)(2,1)S(1)} copy-done((bf16[4,256,256]{2,1,0:T(8,128)(2,1)S(1)}, bf16[4,256,256]{2,1,0:T(8,128)(2,1)}, u32[]{:S(2)}) %copy-start.2) | copy-done | bytes 524312
  4.0 98.4 %gathered_attention.1 = bf16[4,256,256]{2,1,0:T(8,128)(2,1)S(1)} custom-call(s32[16]{0:T(128)S(1)} %copy-done.3, s32[56,45]{1,0:T(8,128)S(1)} %copy.6.listed_ref, bf16[4,256,256]{2,1,0:T(8,128)(2,1)S(1)} %copy-done, bf16[4,256,256]{2,1,0:T(8,128)(2,1)S(1)} %copy-done.1, bf16[4,256,256]{2,1,0:T(8,128)(2,1)S(1)} %copy-done.2), custom_call_target="tpu_custom_call" | custom-call | flops 17179869184 | bytes 2097152 | tf_op jit(solution)/shard_map/gathered_attention/pallas_call | solution.py:341
  102.4 0.8 copy.8
Async XLA Ops:
  0.0 0.8 copy-start.3
  0.8 1.0 %copy-start = (bf16[4,256,256]{2,1,0:T(8,128)(2,1)S(1)}, bf16[4,256,256]{2,1,0:T(8,128)(2,1)}, u32[]{:S(2)}) copy-start(bf16[4,256,256]{2,1,0:T(8,128)(2,1)} %q_ref.1) | copy-start | bytes 1572868
  1.9 1.0 %copy-start.1 = (bf16[4,256,256]{2,1,0:T(8,128)(2,1)S(1)}, bf16[4,256,256]{2,1,0:T(8,128)(2,1)}, u32[]{:S(2)}) copy-start(bf16[4,256,256]{2,1,0:T(8,128)(2,1)} %k_ref.1) | copy-start | bytes 1572868
  2.9 1.0 %copy-start.2 = (bf16[4,256,256]{2,1,0:T(8,128)(2,1)S(1)}, bf16[4,256,256]{2,1,0:T(8,128)(2,1)}, u32[]{:S(2)}) copy-start(bf16[4,256,256]{2,1,0:T(8,128)(2,1)} %v_ref.1) | copy-start | bytes 1572868
